TPU v7x, 32 devices: a whole 2x2x4 slice. The times are simulated.
32 devices in a mesh: dp: 4 (over y, x), mp: 8 (over z, core).
Axes of the slice: x: 2, y: 2, z: 4, core: 2. Of those that a mesh axis runs over, the one named last changes fastest.
Arguments:
- hidden: bfloat16 [512, 28672], P(None, 'mp'), may hold values from -0.25 to 0.25
- grad_out: bfloat16 [512, 16384], P('mp', 'dp'), may hold values from -6 to 6
- down_weight: bfloat16 [28672, 16384], P('mp', 'dp'), may hold values from -0.03125 to 0.03125
Outputs:
- grad_hidden: bfloat16 [512, 28672], P('dp', 'mp')
- grad_weight: bfloat16 [28672, 16384], P('mp', 'dp')
All inputs are finite; a program needn't handle non-finite values.
Results may differ from a plain program's by a relative error of at most 0.012.
Values may be sent and summed in bfloat16 or wider, within the bound.
A program may use at most 128 MiB of HBM per device.

v0:
```python
import jax
import jax.numpy as jnp
from jax import lax
from jax.sharding import PartitionSpec as P


def per_device(hidden, grad_out, down_weight):
    grad_panel = lax.all_gather(grad_out, "mp", axis=0, tiled=True)
    grad_weight = lax.dot_general(
        hidden, grad_panel, (((0,), (0,)), ((), ())), preferred_element_type=jnp.float32
    )
    partial_value = lax.dot_general(
        grad_panel, down_weight, (((1,), (1,)), ((), ())), preferred_element_type=jnp.float32
    ).astype(jnp.bfloat16)
    partial_value = lax.optimization_barrier(partial_value)
    grad_hidden = lax.psum_scatter(
        partial_value.astype(jnp.float32).astype(jnp.bfloat16),
        "dp",
        scatter_dimension=0,
        tiled=True,
    )
    return (grad_hidden, grad_weight.astype(jnp.bfloat16))


def solution(mesh):
    return jax.shard_map(
        per_device,
        mesh=mesh,
        in_specs=(P(None, "mp"), P("mp", "dp"), P("mp", "dp")),
        out_specs=(P("dp", "mp"), P("mp", "dp")),
        check_vma=False,
    )
```

profile of v0, /device:TPU:0, one launch (start us, length us, event | category | flops | bytes accessed | tf_op | source)
XLA Modules:
  0.0 136.6 jit_solution(15498748075864960311)
XLA Ops:
  7.2 0.0 all-gather.2.cloned.1.call-start
  7.2 0.7 all-gather.2.cloned.1.call-update
  7.9 0.0 reduce-scatter.2.cloned.1.call-start
  7.9 51.5 %all-gather.2.cloned.1.call-done = bf16[512,4096]{1,0:T(8,128)(2,1)} async-done(((bf16[64,4096]{1,0:T(8,128)(2,1)}), bf16[512,4096]{1,0:T(8,128)(2,1)}) %all-gather.2.cloned.1.call-update) | async-done | bytes 4194320 | tf_op jit(solution)/shard_map/all_gather | solution.py:8
  59.5 23.1 %convolution_convert_fusion.1 = bf16[512,3584]{1,0:T(8,128)(2,1)} fusion(bf16[512,4096]{1,0:T(8,128)(2,1)} %all-gather.2.cloned.1.call-done, bf16[3584,4096]{1,0:T(8,128)(2,1)} %param.5), kind=kOutput, calls=%fused_computation.1 | convolution fusion | flops 15034220544 | bytes 37224448 | tf_op jit(solution)/shard_map/dot_general | solution.py:12
  82.6 0.0 reduce-scatter.2.cloned.1.call-update
  82.6 21.6 %convolution_convert_fusion = bf16[3584,4096]{1,0:T(8,128)(2,1)} fusion(bf16[512,3584]{1,0:T(8,128)(2,1)} %param.3, bf16[512,4096]{1,0:T(8,128)(2,1)} %all-gather.2.cloned.1.call-done), kind=kOutput, calls=%fused_computation | convolution fusion | flops 15047065600 | bytes 37224448 | tf_op jit(solution)/shard_map/dot_general | solution.py:9
  104.2 25.6 %reduce-scatter.2.cloned.1.call-done = bf16[128,3584]{1,0:T(8,128)(2,1)} async-done(((bf16[512,3584]{1,0:T(8,128)(2,1)}), bf16[128,3584]{1,0:T(8,128)(2,1)}) %reduce-scatter.2.cloned.1.call-update) | async-done | bytes 917520 | tf_op jit(solution)/shard_map/reduce_scatter | solution.py:16
Async XLA Ops:
  7.2 52.3 %all-gather.2.cloned.1.call-start = ((), (), s32[]{:S(2)}) async-start(), calls=%async_computation.1 | async-start | bytes 4718592 | tf_op jit(solution)/shard_map/all_gather | solution.py:8
  7.9 121.9 %reduce-scatter.2.cloned.1.call-start = ((), (), s32[]{:S(2)}) async-start(), calls=%async_computation.2 | async-start | bytes 4587520 | tf_op jit(solution)/shard_map/reduce_scatter | solution.py:16
Sparse Core Ops, SparseCore 0:
  9.6 49.8 all-gather.1
  82.7 47.0 reduce-scatter.1
where the time goes:
time: 137 us
  waiting for transfers between devices  77.8 us (57%)
  matrix products  44.7 us (33%)
  between operations  14 us (10%)
    all_gather x1, waiting for transfers between devices, per_device(): grad_panel = lax.all_gather(grad_out, 'mp', axis=0, tiled=True)  51.5 us
    reduce_scatter x1, waiting for transfers between devices, per_device(): lax.psum_scatter(partial_value.astype(jnp.float32).astype(jnp.bfloat16),...  25.6 us
    dot_general x1, matrix products, per_device(): lax.dot_general(grad_panel, down_weight, (((1,), (1,)), ((), ())), prefer...  23.1 us
    dot_general x1, matrix products, per_device(): lax.dot_general(hidden, grad_panel, (((0,), (0,)), ((), ())), preferred_e...  21.6 us
  transfers between devices with their start and end apart: 2, of which 2 were waited for; matrix products, arithmetic and copies ran while one was open for 16% of the time, Pallas kernels for 0%

commit v1 on v0

v1 whole, which is shorter than its diff:
```python
import functools

import jax
import jax.numpy as jnp
from jax import lax
from jax.experimental import pallas as pl
from jax.experimental.pallas import tpu as pltpu
from jax.sharding import PartitionSpec as P

ROWS = 16
MESH = pl.DeviceIdType.MESH


def gather_kernel(n_dp, n_mp, rounds, kernel_rounds, chunk,
                  g_ref, w_ref, panel_out, part_out, gh_out,
                  panel, w, part, arrived,
                  g_sem, w_sem, panel_sem, part_sem,
                  z_send, z_recv, sib_send, sib_recv, rs_send, rs_recv):
    d = lax.axis_index("dp")
    me = lax.axis_index("mp")
    chip = me // 2
    core = lax.rem(me, 2)
    sibling = me + 1 - 2 * core
    chips = n_mp // 2
    per_owner = n_mp // n_dp
    chunks = w.shape[0] // chunk

    g_copy = pltpu.make_async_copy(g_ref, panel.at[:, me], g_sem)
    g_copy.start()

    def w_copy(i):
        rows = pl.ds(pl.multiple_of(i * chunk, chunk), chunk)
        return pltpu.make_async_copy(w_ref.at[rows, :], w.at[rows, :], w_sem.at[i])

    @pl.loop(0, chunks)
    def _(i):
        w_copy(i).start()

    barrier = pltpu.get_barrier_semaphore()

    def greet(dp, mp):
        pl.semaphore_signal(barrier, inc=1, device_id=(dp, mp), device_id_type=MESH)

    greet(d, sibling)

    @pl.when(chip > 0)
    def _():
        greet(d, me - 2)

    @pl.when(chip < chips - 1)
    def _():
        greet(d, me + 2)

    for j in range(n_dp - 1):
        greet(lax.rem(d + j + 1, n_dp), me)
    heard = n_dp + jnp.where(chip > 0, 1, 0) + jnp.where(chip < chips - 1, 1, 0)
    pl.semaphore_wait(barrier, heard)
    g_copy.wait()

    def z_copy(r, way, k, m):
        return pltpu.make_async_remote_copy(
            src_ref=panel.at[r, m], dst_ref=panel.at[r, m],
            send_sem=z_send.at[r, way, k], recv_sem=z_recv.at[r, way, k],
            device_id=(d, me - 2 if way == 0 else me + 2), device_id_type=MESH)

    def sib_copy(r, way, k, m):
        return pltpu.make_async_remote_copy(
            src_ref=panel.at[r, m], dst_ref=panel.at[r, m],
            send_sem=sib_send.at[r, way, k], recv_sem=sib_recv.at[r, way, k],
            device_id=(d, sibling), device_id_type=MESH)

    def further(way):
        return chip > 0 if way == 0 else chip < chips - 1

    def inside(way, k):
        return chip + k < chips if way == 0 else chip - k >= 0

    def source(way, k):
        return chip + k if way == 0 else chip - k

    def send_own(r):
        for way in range(2):
            @pl.when(further(way))
            def _():
                z_copy(r, way, 1, me).start()
        sib_copy(r, 0, 0, me).start()

    def forward(r, k):
        for way in range(2):
            @pl.when(inside(way, k))
            def _():
                m = 2 * source(way, k) + core
                z_copy(r, way, k, m).wait_recv()

                @pl.when(further(way))
                def _():
                    z_copy(r, way, k + 1, m).start()

                sib_copy(r, way, k, m).start()

    def wait_siblings(r):
        sib_copy(r, 0, 0, sibling).wait_recv()

        @pl.loop(1, chips)
        def _(k):
            for way in range(2):
                @pl.when(inside(way, k))
                def _():
                    sib_copy(r, way, k, 2 * source(way, k) + 1 - core).wait_recv()

    def panel_copy(r):
        return pltpu.make_async_copy(panel.at[r], panel_out.at[:, r], panel_sem.at[r])

    def part_copy(r):
        return pltpu.make_async_copy(
            part.at[r], part_out.at[:, r - kernel_rounds], part_sem.at[r])

    def rs_copy(r, j):
        owner = lax.rem(d + j + 1, n_dp)
        return pltpu.make_async_remote_copy(
            src_ref=part.at[r, pl.ds(owner * per_owner, per_owner)],
            dst_ref=arrived.at[j, r],
            send_sem=rs_send.at[j, r], recv_sem=rs_recv.at[j, r],
            device_id=(owner, me), device_id_type=MESH)

    send_own(0)
    if rounds > 1:
        send_own(1)

    @pl.loop(1, chips)
    def _(k):
        forward(0, k)

    def send_part(r):
        @pl.when(r < kernel_rounds)
        def _():
            for j in range(n_dp - 1):
                rs_copy(r, j).start()

        @pl.when(r >= kernel_rounds)
        def _():
            part_copy(r).start()

    groups = chips - 1

    @pl.loop(0, rounds)
    def _(r):
        @pl.when(r + 2 < rounds)
        def _():
            send_own(r + 2)

        wait_siblings(r)
        panel_copy(r).start()

        @pl.loop(0, groups)
        def _(k):
            @pl.loop(chunks * k // groups, chunks * (k + 1) // groups)
            def _(i):
                @pl.when(r == 0)
                def _():
                    w_copy(i).wait()

                cols = pl.ds(pl.multiple_of(i * chunk, chunk), chunk)
                a = panel[r].reshape(n_mp * ROWS, panel.shape[-1])
                out = lax.dot_general(a, w[cols, :], (((1,), (1,)), ((), ())),
                                      preferred_element_type=jnp.float32)
                part[r, :, :, cols] = out.astype(part.dtype).reshape(n_mp, ROWS, chunk)

            @pl.when(k == groups - 1)
            def _():
                send_part(r)

            @pl.when(r + 1 < rounds)
            def _():
                forward(r + 1, k + 1)

    for r in range(kernel_rounds):
        for j in range(n_dp - 1):
            rs_copy(r, j).wait_recv()

        @pl.loop(0, chunks)
        def _(i):
            cols = pl.ds(pl.multiple_of(i * chunk, chunk), chunk)
            total = part[r, pl.ds(d * per_owner, per_owner), :, cols].astype(jnp.float32)
            for j in range(n_dp - 1):
                total += arrived[j, r, :, :, cols].astype(jnp.float32)
            gh_out[:, r, :, cols] = total.astype(gh_out.dtype)

    @pl.loop(0, rounds)
    def _(r):
        panel_copy(r).wait()
        sib_copy(r, 0, 0, me).wait_send()
        for way in range(2):
            @pl.when(further(way))
            def _():
                z_copy(r, way, 1, me).wait_send()

        @pl.loop(1, chips)
        def _(k):
            for way in range(2):
                @pl.when(inside(way, k))
                def _():
                    m = 2 * source(way, k) + core
                    sib_copy(r, way, k, m).wait_send()

                    @pl.when(further(way))
                    def _():
                        z_copy(r, way, k + 1, m).wait_send()

        @pl.when(r < kernel_rounds)
        def _():
            for j in range(n_dp - 1):
                rs_copy(r, j).wait_send()

        @pl.when(r >= kernel_rounds)
        def _():
            part_copy(r).wait()


def weight_kernel(tile, h_ref, g_ref, out_ref):
    h = h_ref[...]

    @pl.loop(0, out_ref.shape[1] // tile)
    def _(i):
        cols = pl.ds(pl.multiple_of(i * tile, tile), tile)
        out_ref[:, cols] = lax.dot_general(
            h, g_ref[:, cols], (((0,), (0,)), ((), ())),
            preferred_element_type=jnp.float32).astype(out_ref.dtype)


def weight_gradient(hidden, panel):
    tokens, units = hidden.shape
    width = panel.shape[1]
    block = next(c for c in (256, 128) if units % c == 0)
    return pl.pallas_call(
        functools.partial(weight_kernel, min(width, 1024)),
        grid=(units // block,),
        out_shape=jax.ShapeDtypeStruct((units, width), hidden.dtype),
        in_specs=[
            pl.BlockSpec((tokens, block), lambda i: (0, i)),
            pl.BlockSpec((tokens, width), lambda i: (0, 0)),
        ],
        out_specs=pl.BlockSpec((block, width), lambda i: (i, 0)),
        compiler_params=pltpu.CompilerParams(vmem_limit_bytes=48 * 1024 * 1024),
        cost_estimate=pl.CostEstimate(
            flops=2 * tokens * width * units, transcendentals=0,
            bytes_accessed=2 * units * width),
    )(hidden, panel)


def per_device(n_dp, n_mp, hidden, grad_out, down_weight):
    rows, width = grad_out.shape
    units = down_weight.shape[0]
    tokens = rows * n_mp
    rounds = rows // ROWS
    kernel_rounds = rounds - rounds // 4
    rest = rounds - kernel_rounds
    chips = n_mp // 2
    per_owner = n_mp // n_dp
    chunk = next(c for c in (512, 256, 128) if units % c == 0)
    chunks = units // chunk
    bf16 = jnp.bfloat16
    dma = pltpu.SemaphoreType.DMA

    panel, part, gh = pl.pallas_call(
        functools.partial(gather_kernel, n_dp, n_mp, rounds, kernel_rounds, chunk),
        out_shape=(
            jax.ShapeDtypeStruct((n_mp, rounds, ROWS, width), bf16),
            jax.ShapeDtypeStruct((n_mp, rest, ROWS, units), bf16),
            jax.ShapeDtypeStruct((per_owner, kernel_rounds, ROWS, units), bf16),
        ),
        in_specs=[pl.BlockSpec(memory_space=pl.ANY)] * 2,
        out_specs=(
            pl.BlockSpec(memory_space=pl.ANY),
            pl.BlockSpec(memory_space=pl.ANY),
            pl.BlockSpec(memory_space=pltpu.VMEM),
        ),
        scratch_shapes=[
            pltpu.VMEM((rounds, n_mp, ROWS, width), bf16),
            pltpu.VMEM((units, width), bf16),
            pltpu.VMEM((rounds, n_mp, ROWS, units), bf16),
            pltpu.VMEM((n_dp - 1, kernel_rounds, per_owner, ROWS, units), bf16),
            dma, dma((chunks,)), dma((rounds,)), dma((rounds,)),
            dma((rounds, 2, chips)), dma((rounds, 2, chips)),
            dma((rounds, 2, chips)), dma((rounds, 2, chips)),
            dma((n_dp - 1, kernel_rounds)), dma((n_dp - 1, kernel_rounds)),
        ],
        compiler_params=pltpu.CompilerParams(
            collective_id=0, has_side_effects=True, vmem_limit_bytes=56 * 1024 * 1024),
        cost_estimate=pl.CostEstimate(
            flops=2 * tokens * width * units, transcendentals=0,
            bytes_accessed=2 * units * width),
    )(grad_out.reshape(rounds, ROWS, width), down_weight)

    scattered = lax.psum_scatter(
        part.reshape(n_mp * rest * ROWS, units), "dp", scatter_dimension=0, tiled=True)
    grad_weight = weight_gradient(hidden, panel.reshape(tokens, width))
    grad_hidden = jnp.concatenate(
        [gh.reshape(per_owner, kernel_rounds * ROWS, units),
         scattered.reshape(per_owner, rest * ROWS, units)], axis=1)
    return grad_hidden.reshape(tokens // n_dp, units), grad_weight


def solution(mesh):
    return jax.shard_map(
        functools.partial(per_device, mesh.shape["dp"], mesh.shape["mp"]),
        mesh=mesh,
        in_specs=(P(None, "mp"), P("mp", "dp"), P("mp", "dp")),
        out_specs=(P("dp", "mp"), P("mp", "dp")),
        check_vma=False,
    )
```

time: 137 us -> 119 us (0.87)
  Pallas kernels: 0 us -> 101 us
  waiting for transfers between devices: 77.8 us -> 0.02 us
  matrix products: 44.7 us -> 0 us
  local copies, waits for them, and re-layouts: 0 us -> 2.04 us
  other arithmetic: 0 us -> 1.92 us
    pallas_call x0 -> x2, Pallas kernels: none -> 101 us  [the longest x1 70.6 us: per_device(): pl.pallas_call(functools.partial(gather_kernel, n_dp, n_mp, rounds, kerne...]
    all_gather x1 -> x0, waiting for transfers between devices: 51.5 us -> none  [per_device(): grad_panel = lax.all_gather(grad_out, 'mp', axis=0, tiled=True)]
    dot_general x2 -> x0, matrix products: 44.7 us -> none  [the longest x1 23.1 us: per_device(): lax.dot_general(grad_panel, down_weight, (((1,), (1,)), ((), ())), prefer...]
    reduce_scatter x1, waiting for transfers between devices: 25.6 us -> 0.01 us  [per_device(): lax.psum_scatter(part.reshape(n_mp * rest * ROWS, units), 'dp', scatter_d...]
    unnamed x0 -> x4, local copies, waits for them, and re-layouts: none -> 2.04 us
    concatenate x0 -> x1, other arithmetic: none -> 1.92 us  [per_device(): jnp.concatenate([gh.reshape(per_owner, kernel_rounds * ROWS, units), scat...]
  transfers between devices with their start and end apart: 2 -> 1, of which waited for: 2 -> 0; matrix products, arithmetic and copies ran while one was open for 16% -> 0% of each run, Pallas kernels for 0% -> 26%
where the time goes in v1:
time: 119 us
  Pallas kernels  101 us (85%)
  between operations  14 us (12%)
  local copies, waits for them, and re-layouts  2.04 us (2%)
  other arithmetic  1.92 us (2%)
    pallas_call x1, Pallas kernels, per_device(): pl.pallas_call(functools.partial(gather_kernel, n_dp, n_mp, rounds, kerne...  70.6 us
    pallas_call x1, Pallas kernels, weight_gradient(): pl.pallas_call(functools.partial(weight_kernel, min(width, 1024)), grid=(...  30.5 us
  transfers between devices with their start and end apart: 1, of which 0 were waited for; matrix products, arithmetic and copies ran while one was open for 0% of the time, Pallas kernels for 26%

profile of v1, /device:TPU:0, one launch (start us, length us, event | category | flops | bytes accessed | tf_op | source)
XLA Modules:
  0.0 119.1 jit_solution(5649487405236806775)
XLA Ops:
  7.2 0.0 reduce-scatter.2.cloned.1.call-start
  7.2 70.6 %shard_map.50 = (bf16[8,4,16,4096]{3,2,1,0:T(8,128)(2,1)}, bf16[8,1,16,3584]{3,2,1,0:T(8,128)(2,1)}, bf16[2,3,16,3584]{3,2,1,0:T(8,128)(2,1)}) custom-call(bf16[4,16,4096]{2,1,0:T(8,128)(2,1)} %bitcast.10, bf16[3584,4096]{1,0:T(8,128)(2,1)} %w_ref.1), custom_call_target="tpu_custom_call" | custom-call | flops 15032385536 | bytes 29360128 | tf_op jit(solution)/shard_map/pallas_call | solution.py:265
  77.8 0.0 reduce-scatter.2.cloned.1.call-update
  77.8 0.0 copy-start
  77.9 2.0 %copy-done = bf16[512,3584]{1,0:T(8,128)(2,1)S(1)} copy-done((bf16[512,3584]{1,0:T(8,128)(2,1)S(1)}, bf16[512,3584]{1,0:T(8,128)(2,1)}, u32[]{:S(2)}) %copy-start) | copy-done | bytes 3670040
  79.9 0.0 copy-start.1
  79.9 30.5 %shard_map.51 = bf16[3584,4096]{1,0:T(8,128)(2,1)} custom-call(bf16[512,3584]{1,0:T(8,128)(2,1)S(1)} %copy-done, bf16[512,4096]{1,0:T(8,128)(2,1)} %bitcast.11), custom_call_target="tpu_custom_call" | custom-call | flops 15032385536 | bytes 29360128 | tf_op jit(solution)/shard_map/pallas_call | solution.py:235
  110.3 0.0 reduce-scatter.2.cloned.1.call-done
  110.4 0.0 copy-done.1
  110.4 1.9 %pad_maximum_fusion = bf16[2,64,3584]{2,1,0:T(8,128)(2,1)} fusion(bf16[2,16,3584]{2,1,0:T(8,128)(2,1)} %bitcast.9, bf16[2,48,3584]{2,1,0:T(8,128)(2,1)S(1)} %bitcast.8), kind=kLoop, calls=%fused_computation | loop fusion | flops 1835008 | bytes 1835008 | tf_op jit(solution)/shard_map/concatenate | solution.py:298
Async XLA Ops:
  7.2 103.2 %reduce-scatter.2.cloned.1.call-start = ((), (), s32[]{:S(2)}) async-start(), calls=%async_computation.1 | async-start | bytes 1146880 | tf_op jit(solution)/shard_map/reduce_scatter | solution.py:295
  77.8 2.0 %copy-start = (bf16[512,3584]{1,0:T(8,128)(2,1)S(1)}, bf16[512,3584]{1,0:T(8,128)(2,1)}, u32[]{:S(2)}) copy-start(bf16[512,3584]{1,0:T(8,128)(2,1)} %h_ref.1) | copy-start | bytes 11010052
  79.9 30.5 %copy-start.1 = (bf16[2,3,16,3584]{3,2,1,0:T(8,128)(2,1)S(1)}, bf16[2,3,16,3584]{3,2,1,0:T(8,128)(2,1)}, u32[]{:S(2)}) copy-start(bf16[2,3,16,3584]{3,2,1,0:T(8,128)(2,1)} %get-tuple-element.5) | copy-start | bytes 2064388
Sparse Core Ops, SparseCore 0:
  78.0 25.3 reduce-scatter.1

commit v2 on v1

--- a/solution.py
+++ b/solution.py
@@ -7,14 +7,14 @@
 from jax.experimental.pallas import tpu as pltpu
 from jax.sharding import PartitionSpec as P
 
-ROWS = 16
+ROWS = 32
 MESH = pl.DeviceIdType.MESH
 
 
-def gather_kernel(n_dp, n_mp, rounds, kernel_rounds, chunk,
-                  g_ref, w_ref, panel_out, part_out, gh_out,
+def gather_kernel(n_dp, n_mp, rounds, chunk,
+                  g_ref, w_ref, panel_out, gh_out,
                   panel, w, part, arrived,
-                  g_sem, w_sem, panel_sem, part_sem,
+                  g_sem, w_sem, panel_sem,
                   z_send, z_recv, sib_send, sib_recv, rs_send, rs_recv):
     d = lax.axis_index("dp")
     me = lax.axis_index("mp")
@@ -111,16 +111,13 @@
     def panel_copy(r):
         return pltpu.make_async_copy(panel.at[r], panel_out.at[:, r], panel_sem.at[r])
 
-    def part_copy(r):
-        return pltpu.make_async_copy(
-            part.at[r], part_out.at[:, r - kernel_rounds], part_sem.at[r])
-
-    def rs_copy(r, j):
+    def rs_copy(r, j, i):
+        cols = pl.ds(pl.multiple_of(i * chunk, chunk), chunk)
         owner = lax.rem(d + j + 1, n_dp)
         return pltpu.make_async_remote_copy(
-            src_ref=part.at[r, pl.ds(owner * per_owner, per_owner)],
-            dst_ref=arrived.at[j, r],
-            send_sem=rs_send.at[j, r], recv_sem=rs_recv.at[j, r],
+            src_ref=part.at[r, pl.ds(owner * per_owner, per_owner), :, cols],
+            dst_ref=arrived.at[j, r, :, :, cols],
+            send_sem=rs_send.at[j, r, i], recv_sem=rs_recv.at[j, r, i],
             device_id=(owner, me), device_id_type=MESH)
 
     send_own(0)
@@ -130,16 +127,6 @@
     @pl.loop(1, chips)
     def _(k):
         forward(0, k)
-
-    def send_part(r):
-        @pl.when(r < kernel_rounds)
-        def _():
-            for j in range(n_dp - 1):
-                rs_copy(r, j).start()
-
-        @pl.when(r >= kernel_rounds)
-        def _():
-            part_copy(r).start()
 
     groups = chips - 1
 
@@ -165,21 +152,18 @@
                 out = lax.dot_general(a, w[cols, :], (((1,), (1,)), ((), ())),
                                       preferred_element_type=jnp.float32)
                 part[r, :, :, cols] = out.astype(part.dtype).reshape(n_mp, ROWS, chunk)
-
-            @pl.when(k == groups - 1)
-            def _():
-                send_part(r)
+                for j in range(n_dp - 1):
+                    rs_copy(r, j, i).start()
 
             @pl.when(r + 1 < rounds)
             def _():
                 forward(r + 1, k + 1)
 
-    for r in range(kernel_rounds):
-        for j in range(n_dp - 1):
-            rs_copy(r, j).wait_recv()
-
+    for r in range(rounds):
         @pl.loop(0, chunks)
         def _(i):
+            for j in range(n_dp - 1):
+                rs_copy(r, j, i).wait_recv()
             cols = pl.ds(pl.multiple_of(i * chunk, chunk), chunk)
             total = part[r, pl.ds(d * per_owner, per_owner), :, cols].astype(jnp.float32)
             for j in range(n_dp - 1):
@@ -207,33 +191,29 @@
                     def _():
                         z_copy(r, way, k + 1, m).wait_send()
 
-        @pl.when(r < kernel_rounds)
-        def _():
+        @pl.loop(0, chunks)
+        def _(i):
             for j in range(n_dp - 1):
-                rs_copy(r, j).wait_send()
-
-        @pl.when(r >= kernel_rounds)
-        def _():
-            part_copy(r).wait()
-
-
-def weight_kernel(tile, h_ref, g_ref, out_ref):
-    h = h_ref[...]
+                rs_copy(r, j, i).wait_send()
+
+
+def weight_kernel(tile, h_ref, g_ref, out_ref, h):
+    h[...] = h_ref[...].T
 
     @pl.loop(0, out_ref.shape[1] // tile)
     def _(i):
         cols = pl.ds(pl.multiple_of(i * tile, tile), tile)
         out_ref[:, cols] = lax.dot_general(
-            h, g_ref[:, cols], (((0,), (0,)), ((), ())),
+            h[...], g_ref[:, cols], (((1,), (0,)), ((), ())),
             preferred_element_type=jnp.float32).astype(out_ref.dtype)
 
 
 def weight_gradient(hidden, panel):
     tokens, units = hidden.shape
     width = panel.shape[1]
-    block = next(c for c in (256, 128) if units % c == 0)
+    block = next(c for c in (512, 256, 128) if units % c == 0)
     return pl.pallas_call(
-        functools.partial(weight_kernel, min(width, 1024)),
+        functools.partial(weight_kernel, min(width, 512)),
         grid=(units // block,),
         out_shape=jax.ShapeDtypeStruct((units, width), hidden.dtype),
         in_specs=[
@@ -241,7 +221,8 @@
             pl.BlockSpec((tokens, width), lambda i: (0, 0)),
         ],
         out_specs=pl.BlockSpec((block, width), lambda i: (i, 0)),
-        compiler_params=pltpu.CompilerParams(vmem_limit_bytes=48 * 1024 * 1024),
+        scratch_shapes=[pltpu.VMEM((block, tokens), hidden.dtype)],
+        compiler_params=pltpu.CompilerParams(vmem_limit_bytes=61 * 1024 * 1024),
         cost_estimate=pl.CostEstimate(
             flops=2 * tokens * width * units, transcendentals=0,
             bytes_accessed=2 * units * width),
@@ -253,8 +234,6 @@
     units = down_weight.shape[0]
     tokens = rows * n_mp
     rounds = rows // ROWS
-    kernel_rounds = rounds - rounds // 4
-    rest = rounds - kernel_rounds
     chips = n_mp // 2
     per_owner = n_mp // n_dp
     chunk = next(c for c in (512, 256, 128) if units % c == 0)
@@ -262,16 +241,14 @@
     bf16 = jnp.bfloat16
     dma = pltpu.SemaphoreType.DMA
 
-    panel, part, gh = pl.pallas_call(
-        functools.partial(gather_kernel, n_dp, n_mp, rounds, kernel_rounds, chunk),
+    panel, gh = pl.pallas_call(
+        functools.partial(gather_kernel, n_dp, n_mp, rounds, chunk),
         out_shape=(
             jax.ShapeDtypeStruct((n_mp, rounds, ROWS, width), bf16),
-            jax.ShapeDtypeStruct((n_mp, rest, ROWS, units), bf16),
-            jax.ShapeDtypeStruct((per_owner, kernel_rounds, ROWS, units), bf16),
+            jax.ShapeDtypeStruct((per_owner, rounds, ROWS, units), bf16),
         ),
         in_specs=[pl.BlockSpec(memory_space=pl.ANY)] * 2,
         out_specs=(
-            pl.BlockSpec(memory_space=pl.ANY),
             pl.BlockSpec(memory_space=pl.ANY),
             pl.BlockSpec(memory_space=pltpu.VMEM),
         ),
@@ -279,11 +256,11 @@
             pltpu.VMEM((rounds, n_mp, ROWS, width), bf16),
             pltpu.VMEM((units, width), bf16),
             pltpu.VMEM((rounds, n_mp, ROWS, units), bf16),
-            pltpu.VMEM((n_dp - 1, kernel_rounds, per_owner, ROWS, units), bf16),
-            dma, dma((chunks,)), dma((rounds,)), dma((rounds,)),
+            pltpu.VMEM((n_dp - 1, rounds, per_owner, ROWS, units), bf16),
+            dma, dma((chunks,)), dma((rounds,)),
             dma((rounds, 2, chips)), dma((rounds, 2, chips)),
             dma((rounds, 2, chips)), dma((rounds, 2, chips)),
-            dma((n_dp - 1, kernel_rounds)), dma((n_dp - 1, kernel_rounds)),
+            dma((n_dp - 1, rounds, chunks)), dma((n_dp - 1, rounds, chunks)),
         ],
         compiler_params=pltpu.CompilerParams(
             collective_id=0, has_side_effects=True, vmem_limit_bytes=56 * 1024 * 1024),
@@ -292,13 +269,8 @@
             bytes_accessed=2 * units * width),
     )(grad_out.reshape(rounds, ROWS, width), down_weight)
 
-    scattered = lax.psum_scatter(
-        part.reshape(n_mp * rest * ROWS, units), "dp", scatter_dimension=0, tiled=True)
     grad_weight = weight_gradient(hidden, panel.reshape(tokens, width))
-    grad_hidden = jnp.concatenate(
-        [gh.reshape(per_owner, kernel_rounds * ROWS, units),
-         scattered.reshape(per_owner, rest * ROWS, units)], axis=1)
-    return grad_hidden.reshape(tokens // n_dp, units), grad_weight
+    return gh.reshape(tokens // n_dp, units), grad_weight
 
 
 def solution(mesh):

time: 119 us -> 108 us (0.908)
  between operations: 14 us -> 0.65 us
  Pallas kernels: 101 us -> 105 us
  other arithmetic: 1.92 us -> 0 us
    pallas_call x2, Pallas kernels: 101 us -> 105 us  [the longest x1 74.7 us: per_device(): pl.pallas_call(functools.partial(gather_kernel, n_dp, n_mp, rounds, chunk...]
    concatenate x1 -> x0, other arithmetic: 1.92 us -> none  [per_device(): jnp.concatenate([gh.reshape(per_owner, kernel_rounds * ROWS, units), scat...]
  transfers between devices with their start and end apart: 1 -> 0, of which waited for: 0 -> 0; matrix products, arithmetic and copies ran while one was open for 0% -> 0% of each run, Pallas kernels for 26% -> 0%
where the time goes in v2:
time: 108 us; the launch traced here: 107 us
  Pallas kernels  105 us (97%)
    pallas_call x1, Pallas kernels, per_device(): pl.pallas_call(functools.partial(gather_kernel, n_dp, n_mp, rounds, chunk...  74.7 us
    pallas_call x1, Pallas kernels, weight_gradient(): pl.pallas_call(functools.partial(weight_kernel, min(width, 512)), grid=(u...  30.6 us

profile of v2, /device:TPU:0, one launch (start us, length us, event | category | flops | bytes accessed | tf_op | source)
XLA Modules:
  0.0 106.9 jit_solution(6896183777191811949)
XLA Ops:
  0.6 74.7 %shard_map.50 = (bf16[8,2,32,4096]{3,2,1,0:T(8,128)(2,1)}, bf16[2,2,32,3584]{3,2,1,0:T(8,128)(2,1)}) custom-call(bf16[2,32,4096]{2,1,0:T(8,128)(2,1)} %bitcast.4, bf16[3584,4096]{1,0:T(8,128)(2,1)} %w_ref.1), custom_call_target="tpu_custom_call" | custom-call | flops 15032385536 | bytes 29360128 | tf_op jit(solution)/shard_map/pallas_call | solution.py:244
  75.4 0.0 copy-start
  75.4 30.6 %shard_map.51 = bf16[3584,4096]{1,0:T(8,128)(2,1)} custom-call(bf16[512,3584]{1,0:T(8,128)(2,1)} %h_ref.1, bf16[512,4096]{1,0:T(8,128)(2,1)} %bitcast.5), custom_call_target="tpu_custom_call" | custom-call | flops 15032385536 | bytes 29360128 | tf_op jit(solution)/shard_map/pallas_call | solution.py:215
  106.0 0.0 copy-done
  106.0 0.9 copy.6
Async XLA Ops:
  75.4 30.7 %copy-start = (bf16[2,2,32,3584]{3,2,1,0:T(8,128)(2,1)S(1)}, bf16[2,2,32,3584]{3,2,1,0:T(8,128)(2,1)}, u32[]{:S(2)}) copy-start(bf16[2,2,32,3584]{3,2,1,0:T(8,128)(2,1)} %get-tuple-element.4) | copy-start | bytes 2752516
